TPU v7x, 128 devices: a whole 4x4x4 slice. The times are simulated.
128 devices in a mesh: row: 16 (over z_hi, x, core), col: 8 (over z_lo, y).
Axes of the slice: x: 4, y: 4, z: 4 (z_hi: 2, z_lo: 2; z = z_hi * 2 + z_lo), core: 2. Of those that a mesh axis runs over, the one named last changes fastest.
Arguments:
- doubles: bfloat16 [3600, 3840], P('row', 'col'), may hold values from -6 to 6
- singles: float32 [60, 480], replicated, may hold values from -3 to 3
- integrals: bfloat16 [3840, 32768], P(None, ('col', 'row')), may hold values from -0.09375 to 0.09375
Outputs:
- ladder: bfloat16 [3600, 32768], P('row', 'col')
All inputs are finite; a program needn't handle non-finite values.
Results may differ from a plain program's by a relative error of at most 0.005.
Values may be sent and summed in bfloat16 or wider, within the bound.
A program may use at most 128 MiB of HBM per device.

v0:
```python
import jax
import jax.numpy as jnp
from jax import lax
from jax.sharding import PartitionSpec as P


def onehot_rows(index, count):
    return (index[:, None] == jnp.arange(count, dtype=jnp.int32)[None, :]).astype(jnp.float32)


def build_tau(doubles, singles):
    pair_rows = doubles.shape[0]
    pair_cols = doubles.shape[1]
    occupied = singles.shape[0]
    virtual = singles.shape[1]
    global_row = lax.axis_index("row") * pair_rows + jnp.arange(pair_rows, dtype=jnp.int32)
    global_col = lax.axis_index("col") * pair_cols + jnp.arange(pair_cols, dtype=jnp.int32)
    first_occ = onehot_rows(global_row // occupied, occupied)
    second_occ = onehot_rows(global_row % occupied, occupied)
    first_vir = onehot_rows(global_col // virtual, virtual).T
    second_vir = onehot_rows(global_col % virtual, virtual).T
    exact = lax.Precision.HIGHEST
    left = jnp.dot(jnp.dot(first_occ, singles, precision=exact), first_vir, precision=exact)
    right = jnp.dot(jnp.dot(second_occ, singles, precision=exact), second_vir, precision=exact)
    return (doubles.astype(jnp.float32) + left * right).astype(jnp.bfloat16)


def on_device(doubles, singles, integrals):
    tau_local = build_tau(doubles, singles)
    tau_rows = lax.all_gather(tau_local, "col", axis=1, tiled=True)
    grid_block = lax.all_to_all(integrals, "row", split_axis=0, concat_axis=1, tiled=True)
    summed = jnp.dot(
        tau_rows,
        lax.all_gather(grid_block, "row", axis=0, tiled=True),
        preferred_element_type=jnp.float32,
    )
    return summed.astype(jnp.bfloat16)


def solution(mesh):
    in_specs = (P("row", "col"), P(), P(None, ("col", "row")))
    out_specs = P("row", "col")
    return jax.shard_map(
        on_device, mesh=mesh, in_specs=in_specs, out_specs=out_specs, check_vma=False
    )
```

profile of v0, /device:TPU:0, one launch (start us, length us, event | category | flops | bytes accessed | tf_op | source)
XLA Modules:
  0.0 265.0 jit_solution(14303256013045606890)
XLA Ops:
  6.5 0.0 copy-start
  6.5 0.0 copy-start.2
  6.5 0.0 copy-start.1
  6.5 0.0 all-gather.6.cloned.1.call-start
  6.6 0.8 copy-done
  7.4 0.4 fusion.7
  7.8 0.4 fusion.6
  8.2 0.7 fusion.3
  9.0 0.0 copy-done.2
  9.0 1.5 fusion.2
  10.4 0.0 all-gather.6.cloned.1.call-update
  10.5 0.0 all-gather.4.cloned.1.call-start
  10.5 0.0 copy-done.1
  10.5 49.6 %all_to_all.19 = bf16[16,240,256]{2,1,0:T(8,128)(2,1)S(1)} all-to-all(bf16[16,240,256]{2,1,0:T(8,128)(2,1)S(1)} %bitcast.18), channel_id=1, replica_groups=mesh['row'=16,'col'=8] {'row'}, dimensions={0} | all-to-all | bytes 3932160 | tf_op jit(solution)/shard_map/all_to_all | solution.py:31
  60.1 1.5 copy.8
  61.6 0.0 all-gather.4.cloned.1.call-update
  61.7 0.8 all-gather.6.cloned.1.call-done
  62.4 2.1 copy.6
  64.5 4.2 %reshape.40 = bf16[3840,225]{0,1:T(8,128)(2,1)} reshape(bf16[8,480,225]{1,0,2:T(8,128)(2,1)S(1)} %copy.6) | data formatting | bytes 3456000
  68.8 174.1 %all-gather.4.cloned.1.call-done = bf16[3840,4096]{1,0:T(8,128)(2,1)} async-done(((bf16[240,4096]{1,0:T(8,128)(2,1)}), bf16[3840,4096]{1,0:T(8,128)(2,1)}) %all-gather.4.cloned.1.call-update) | async-done | bytes 31457296 | tf_op jit(solution)/shard_map/all_gather | solution.py:34
  242.9 15.2 %convolution_convert_fusion = bf16[225,4096]{1,0:T(8,128)(2,1)} fusion(bf16[3840,225]{0,1:T(8,128)(2,1)} %reshape.40, bf16[3840,4096]{1,0:T(8,128)(2,1)} %all-gather.4.cloned.1.call-done), kind=kOutput, calls=%fused_computation | convolution fusion | flops 7078809600 | bytes 35028480 | tf_op jit(solution)/shard_map/dot_general | solution.py:32
  (2 shorter events, 0.0 us)
Async XLA Ops:
  6.5 0.9 copy-start
  6.5 2.4 copy-start.2
  6.5 4.0 %copy-start.1 = (bf16[3840,256]{1,0:T(8,128)(2,1)S(1)}, bf16[3840,256]{1,0:T(8,128)(2,1)}, u32[]{:S(2)}) copy-start(bf16[3840,256]{1,0:T(8,128)(2,1)} %param.5) | copy-start | bytes 5898244
  6.5 55.9 %all-gather.6.cloned.1.call-start = ((), (), s32[]{:S(2)}) async-start(), calls=%async_computation.2 | async-start | bytes 2138112 | tf_op jit(solution)/shard_map/all_gather | solution.py:30
  10.5 232.4 %all-gather.4.cloned.1.call-start = ((), (), s32[]{:S(2)}) async-start(), calls=%async_computation.1 | async-start | bytes 33423360 | tf_op jit(solution)/shard_map/all_gather | solution.py:34
Sparse Core Ops, SparseCore 0:
  10.6 51.7 all-gather.5
  64.9 177.9 all-gather.3
where the time goes:
time: 266 us; the launch traced here: 265 us
  waiting for transfers between devices  175 us (66%)
  blocking collectives  49.6 us (19%)
  matrix products  18.2 us (7%)
  between operations  13.5 us (5%)
  local copies, waits for them, and re-layouts  8.71 us (3%)
    all_gather x1, waiting for transfers between devices, on_device(): lax.all_gather(grid_block, 'row', axis=0, tiled=True)  174 us
    all_to_all x1, blocking collectives, on_device(): lax.all_to_all(integrals, 'row', split_axis=0, concat_axis=1, tiled=True)  49.6 us
    dot_general x1, matrix products, on_device(): jnp.dot(tau_rows, lax.all_gather(grid_block, 'row', axis=0, tiled=True),...  15.2 us
  transfers between devices with their start and end apart: 2, of which 2 were waited for; matrix products, arithmetic and copies ran while one was open for 3% of the time, Pallas kernels for 0%

commit v1 on v0

v1 whole, which is shorter than its diff:
```python
import functools

import jax
import jax.numpy as jnp
from jax import lax
from jax.experimental import pallas as pl
from jax.experimental.pallas import tpu as pltpu
from jax.sharding import PartitionSpec as P

MESH = pl.DeviceIdType.MESH
ROWS = 240
CUT = 176
DEPTH = 480
WIDTH = 256
ALL = (0, ROWS)
FIRST = (0, CUT)
SECOND = (CUT, ROWS)
HALVES = {FIRST: ((0, 96), (96, CUT)), SECOND: ((CUT, 208), (208, ROWS))}


def span(rows):
    return pl.ds(rows[0], rows[1] - rows[0])


def build_tau(doubles, singles):
    pair_rows, pair_cols = doubles.shape
    occupied = singles.shape[0]
    row, col = lax.axis_index("row"), lax.axis_index("col")
    pairs = occupied * occupied
    tiled = jnp.tile(singles, (pair_rows // occupied + 2, 1))
    right = lax.dynamic_slice(tiled, (lax.rem(row * pair_rows, occupied), 0), (pair_rows, pair_cols))
    column = lax.dynamic_slice(singles, (0, col), (occupied, 1))
    every = jnp.broadcast_to(column, (occupied, occupied)).reshape(pairs)
    left = lax.dynamic_slice(every, (row * pair_rows,), (pair_rows,))
    tau = doubles.astype(jnp.float32) + left[:, None] * right
    return jnp.pad(tau, ((0, ROWS - pair_rows), (0, 0))).astype(jnp.bfloat16)


def kernel(tau_ref, b_ref, out_ref, a, b, c, send_sem, recv_sem, local_sem):
    row, col = lax.axis_index("row"), lax.axis_index("col")
    zh, x, core = row // 8, lax.rem(row // 2, 4), lax.rem(row, 2)
    zl, y = col // 4, lax.rem(col, 4)
    zo = 1 - zl

    def at(dx=0, dy=0, dh=0, dl=0, dc=0):
        return (
            lax.rem(zh + dh, 2) * 8 + lax.rem(x + dx, 4) * 2 + lax.rem(core + dc, 2),
            lax.rem(zl + dl, 2) * 4 + lax.rem(y + dy, 4),
        )

    xs = [lax.rem(x + d, 4) for d in range(4)]
    ys = [lax.rem(y + d, 4) for d in range(4)]
    peers = [at(dx=1), at(dx=2), at(dx=3), at(dy=1), at(dy=3), at(dl=1), at(dh=1), at(dc=1)]

    barrier = pltpu.get_barrier_semaphore()
    for peer in peers:
        pl.semaphore_signal(barrier, inc=1, device_id=peer, device_id_type=MESH)
    pl.semaphore_wait(barrier, len(peers))

    copies = []

    def send(src, dst, device):
        number = len(copies)
        copy = pltpu.make_async_remote_copy(
            src_ref=src,
            dst_ref=dst,
            send_sem=send_sem.at[number],
            recv_sem=recv_sem.at[number],
            device_id=device,
            device_id_type=MESH,
        )
        copy.start()
        copies.append(copy)
        return copy

    def send_a(index, rows, device):
        ref = a.at[index + (span(rows),)]
        return send(ref, ref, device)

    def y_start(dx, lo, rows):
        index = (xs[dx], ys[0], lo)
        return [send_a(index, rows, at(dy=1)), send_a(index, rows, at(dy=3))]

    def y_pass(started, dx, lo, rows, flip):
        up, down = HALVES[rows][::-1] if flip else HALVES[rows]
        for copy in started:
            copy.wait_recv()
        return [
            send_a((xs[dx], ys[3], lo), up, at(dy=1)),
            send_a((xs[dx], ys[1], lo), down, at(dy=3)),
        ]

    def x_start(dy, lo, rows):
        index = (xs[0], ys[dy], lo)
        return [send_a(index, rows, at(dx=1)), send_a(index, rows, at(dx=3))]

    def x_pass(started, dy, lo, rows, flip):
        up, down = HALVES[rows][::-1] if flip else HALVES[rows]
        for copy in started:
            copy.wait_recv()
        return [
            send_a((xs[3], ys[dy], lo), up, at(dx=1)),
            send_a((xs[1], ys[dy], lo), down, at(dx=3)),
        ]

    def arrive(started):
        for copy in started:
            copy.wait_recv()

    both = pl.ds(0, 2)

    def product(dx, half, q):
        total = None
        for lo in range(2):
            for yy in range(4):
                term = jnp.dot(
                    a[xs[dx], yy, lo],
                    b[half, q, pl.ds((lo * 4 + yy) * DEPTH, DEPTH), :],
                    preferred_element_type=jnp.float32,
                )
                total = term if total is None else total + term
        c[dx, half * 2 + q] = total.astype(jnp.bfloat16)

    def own_columns(dx):
        @pl.loop(0, 2)
        def _(q):
            product(dx, 0, q)

    def other_columns(dx, q):
        product(dx, 1, q)

    results = []

    def place(half, q, count):
        return out_ref.at[pl.ds(lax.rem(zh + half, 2) * 8 + x * 2 + q, count)]

    def send_c(dx, half, q, count):
        src = c.at[dx, pl.ds(half * 2 + q, count)]
        results.append(send(src, place(half, q, count), at(dx=dx)))

    mine = pltpu.make_async_copy(b_ref, b.at[0, core], local_sem.at[0])
    mine.start()
    sibling = send(b_ref, b.at[0, core], at(dc=1))

    a[x, y, zl] = tau_ref[...]
    pair = send_a((xs[0], ys[0], zl), ALL, at(dl=1))
    x_o = x_start(0, zl, FIRST)
    y_0o = y_start(0, zl, FIRST)
    y_so = y_start(0, zl, SECOND)

    depth = b.shape[2] // 2
    part = pl.ds(pl.multiple_of(core * depth, depth), depth)
    mine.wait()
    sibling.wait_recv()
    columns = [send(b.at[0, 0, part], b.at[1, 0, part], at(dh=1))]

    x_o2 = x_pass(x_o, 0, zl, FIRST, False)
    pair.wait_recv()
    x_p = x_start(0, zo, FIRST)
    y_sp = y_start(0, zo, SECOND)
    y_0o2 = y_pass(y_0o, 0, zl, FIRST, False)
    y_so2 = y_pass(y_so, 0, zl, SECOND, False)
    arrive(x_o2)
    y_2o = y_start(2, zl, FIRST)
    x_p2 = x_pass(x_p, 0, zo, FIRST, True)
    y_sp2 = y_pass(y_sp, 0, zo, SECOND, True)
    x_s = {}
    x_s[0, 0] = x_start(0, zl, SECOND)
    x_s[0, 1] = x_start(0, zo, SECOND)
    arrive(x_p2)
    y_2p = y_start(2, zo, FIRST)
    x_t = {}
    x_t[0, 0] = x_pass(x_s[0, 0], 0, zl, SECOND, False)
    x_t[0, 1] = x_pass(x_s[0, 1], 0, zo, SECOND, True)
    for dy in (1, 3):
        x_s[dy, 0] = x_start(dy, zl, SECOND)
        x_s[dy, 1] = x_start(dy, zo, SECOND)
    y_2o2 = y_pass(y_2o, 2, zl, FIRST, False)
    y_1o = y_start(1, zl, FIRST)
    for dy in (1, 3):
        x_t[dy, 0] = x_pass(x_s[dy, 0], dy, zl, SECOND, False)
        x_t[dy, 1] = x_pass(x_s[dy, 1], dy, zo, SECOND, True)
    arrive(y_so2 + y_sp2)
    x_s[2, 0] = x_start(2, zl, SECOND)
    x_s[2, 1] = x_start(2, zo, SECOND)
    y_2p2 = y_pass(y_2p, 2, zo, FIRST, True)
    y_1p = y_start(1, zo, FIRST)
    x_t[2, 0] = x_pass(x_s[2, 0], 2, zl, SECOND, False)
    x_t[2, 1] = x_pass(x_s[2, 1], 2, zo, SECOND, True)

    columns[0].wait_recv()
    columns.append(send(b.at[0, 1, part], b.at[1, 1, part], at(dh=1)))
    shared = [send(b.at[1, 0, part], b.at[1, 0, part], at(dc=1))]

    y_1o2 = y_pass(y_1o, 1, zl, FIRST, False)
    y_3o = y_start(3, zl, FIRST)
    for key in x_t:
        arrive(x_t[key])
    arrive(y_2o2 + y_2p2)
    own_columns(2)
    send_c(2, 0, 0, 2)
    y_1p2 = y_pass(y_1p, 1, zo, FIRST, True)
    y_3p = y_start(3, zo, FIRST)
    shared[0].wait_recv()
    other_columns(2, 0)
    send_c(2, 1, 0, 1)
    y_3o2 = y_pass(y_3o, 3, zl, FIRST, False)
    y_0p = y_start(0, zo, FIRST)
    arrive(y_1o2 + y_1p2)
    own_columns(1)
    send_c(1, 0, 0, 2)
    other_columns(1, 0)
    send_c(1, 1, 0, 1)
    y_3p2 = y_pass(y_3p, 3, zo, FIRST, True)
    y_0p2 = y_pass(y_0p, 0, zo, FIRST, True)
    columns[1].wait_recv()
    shared.append(send(b.at[1, 1, part], b.at[1, 1, part], at(dc=1)))
    arrive(y_3o2 + y_3p2)
    own_columns(3)
    send_c(3, 0, 0, 2)
    other_columns(3, 0)
    send_c(3, 1, 0, 1)
    shared[1].wait_recv()
    for dx in (2, 3, 1):
        other_columns(dx, 1)
        send_c(dx, 1, 1, 1)
    arrive(y_0o2 + y_0p2)
    own_columns(0)
    other_columns(0, 0)
    other_columns(0, 1)
    kept = [
        pltpu.make_async_copy(c.at[0, pl.ds(half * 2, 2)], place(half, 0, 2), local_sem.at[1 + half])
        for half in range(2)
    ]
    for copy in kept:
        copy.start()
    for copy in kept:
        copy.wait()
    for copy in results:
        copy.wait_recv()
    for copy in copies:
        copy.wait_send()


def on_device(doubles, singles, integrals):
    rows = doubles.shape[0]
    depth, width = integrals.shape
    blocks = pl.pallas_call(
        kernel,
        out_shape=jax.ShapeDtypeStruct((16, ROWS, width), jnp.bfloat16),
        in_specs=[pl.BlockSpec(memory_space=pltpu.VMEM), pl.BlockSpec(memory_space=pl.ANY)],
        out_specs=pl.BlockSpec(memory_space=pl.ANY),
        scratch_shapes=[
            pltpu.VMEM((4, 4, 2, ROWS, DEPTH), jnp.bfloat16),
            pltpu.VMEM((2, 2, depth, width), jnp.bfloat16),
            pltpu.VMEM((4, 4, ROWS, width), jnp.bfloat16),
            pltpu.SemaphoreType.DMA((128,)),
            pltpu.SemaphoreType.DMA((128,)),
            pltpu.SemaphoreType.DMA((3,)),
        ],
        compiler_params=pltpu.CompilerParams(
            collective_id=0, has_side_effects=True, vmem_limit_bytes=48 << 20
        ),
        cost_estimate=pl.CostEstimate(
            flops=2 * rows * depth * 16 * width, bytes_accessed=32 << 20, transcendentals=0
        ),
        name="ladder",
    )(build_tau(doubles, singles), integrals)
    return blocks[:, :rows].transpose(1, 0, 2).reshape(rows, 16 * width)


def solution(mesh):
    return jax.shard_map(
        on_device,
        mesh=mesh,
        in_specs=(P("row", "col"), P(), P(None, ("col", "row"))),
        out_specs=P("row", "col"),
        check_vma=False,
    )
```

time: 266 us -> 81.5 us (0.31)
  waiting for transfers between devices: 175 us -> 0 us
  Pallas kernels: 0 us -> 76.1 us
  blocking collectives: 49.6 us -> 0 us
  matrix products: 18.2 us -> 0 us
  between operations: 13.5 us -> 0.09 us
  local copies, waits for them, and re-layouts: 8.71 us -> 5.11 us
    all_gather x2 -> x0, waiting for transfers between devices: 175 us -> none  [the longest x1 174 us: on_device(): lax.all_gather(grid_block, 'row', axis=0, tiled=True)]
    pallas_call x0 -> x1, Pallas kernels: none -> 76.1 us  [on_device(): pl.pallas_call(kernel, out_shape=jax.ShapeDtypeStruct((16, ROWS, width),...]
    all_to_all x1 -> x0, blocking collectives: 49.6 us -> none  [on_device(): lax.all_to_all(integrals, 'row', split_axis=0, concat_axis=1, tiled=True)]
    dot_general x5 -> x0, matrix products: 18.2 us -> none  [the longest x1 15.2 us: on_device(): jnp.dot(tau_rows, lax.all_gather(grid_block, 'row', axis=0, tiled=True),...]
    unnamed x7 -> x6, local copies, waits for them, and re-layouts: 5.08 us -> 2.21 us
  transfers between devices with their start and end apart: 2 -> 0, of which waited for: 2 -> 0; matrix products, arithmetic and copies ran while one was open for 3% -> 0% of each run, Pallas kernels for 0% -> 0%
where the time goes in v1:
time: 81.5 us; the launch traced here: 81.4 us
  Pallas kernels  76.1 us (93%)
  local copies, waits for them, and re-layouts  5.11 us (6%)
    pallas_call x1, Pallas kernels, on_device(): pl.pallas_call(kernel, out_shape=jax.ShapeDtypeStruct((16, ROWS, width),...  76.1 us
    unnamed x6, local copies, waits for them, and re-layouts  2.21 us

profile of v1, /device:TPU:0, one launch (start us, length us, event | category | flops | bytes accessed | tf_op | source)
XLA Modules:
  0.0 81.4 jit_solution(1280222997292051179)
XLA Ops:
  0.0 0.0 copy-start
  0.0 0.0 copy-start.1
  0.0 1.1 %dynamic-slice_reduce_fusion = f32[60]{0:T(128)S(1)} fusion(f32[60,480]{1,0:T(8,128)} %param.4, s32[]{:T(128)S(6)} %select_n.9), kind=kLoop, calls=%fused_computation.2 | loop fusion | bytes 484 | tf_op jit(solution)/shard_map/dynamic_slice | solution.py:32
  1.1 0.1 broadcast_in_dim.9
  1.2 0.1 reshape.11
  1.3 0.1 dynamic_slice.10
  1.4 1.0 %tile.4 = f32[5,60,480]{2,1,0:T(8,128)S(1)} broadcast(f32[60,480]{1,0:T(8,128)} %param.4), dimensions={1,2} | broadcast | bytes 691200 | tf_op jit(solution)/shard_map/tile | solution.py:30
  2.3 0.1 tile.10
  2.4 0.0 copy-done.1
  2.4 0.1 add_convert_fusion
  2.6 0.0 copy-done
  2.6 76.1 %ladder.1 = bf16[16,240,256]{2,1,0:T(8,128)(2,1)S(1)} custom-call(bf16[240,480]{1,0:T(8,128)(2,1)S(1)} %pad.5.tau_ref, bf16[3840,256]{1,0:T(8,128)(2,1)S(1)} %copy-done), custom_call_target="tpu_custom_call" | custom-call | flops 7077888000 | bytes 33554432 | tf_op jit(solution)/shard_map/ladder/pallas_call | solution.py:248
  78.7 0.1 slice_bitcast_fusion
  78.8 0.4 copy.4
  79.2 0.1 pad.6
  79.3 2.1 %copy.5 = bf16[29,8,16,256]{3,1,2,0:T(8,128)(2,1)} copy(bf16[29,8,16,256]{3,2,1,0:T(8,128)(2,1)S(1)} %bitcast.5) | data formatting | bytes 3801088
  (1 shorter events, 0.0 us)
Async XLA Ops:
  0.0 2.6 %copy-start = (bf16[3840,256]{1,0:T(8,128)(2,1)S(1)}, bf16[3840,256]{1,0:T(8,128)(2,1)}, u32[]{:S(2)}) copy-start(bf16[3840,256]{1,0:T(8,128)(2,1)} %b_ref.1) | copy-start | bytes 5898244
  0.0 2.4 %copy-start.1 = (bf16[225,480]{1,0:T(8,128)(2,1)S(1)}, bf16[225,480]{1,0:T(8,128)(2,1)}, u32[]{:S(2)}) copy-start(bf16[225,480]{1,0:T(8,128)(2,1)} %param.3) | copy-start | bytes 648004

commit v2 on v1

v2 whole, which is shorter than its diff:
```python
import math

import jax
import jax.numpy as jnp
from jax import lax
from jax.experimental import pallas as pl
from jax.experimental.pallas import tpu as pltpu
from jax.sharding import PartitionSpec as P

MESH = pl.DeviceIdType.MESH
ROWS = 240
CUT = 176
DEPTH = 480
WIDTH = 256
ALL = (0, ROWS)
FIRST = (0, CUT)
SECOND = (CUT, ROWS)
HALVES = {FIRST: ((0, 96), (96, CUT)), SECOND: ((CUT, 208), (208, ROWS))}


def span(rows):
    return pl.ds(rows[0], rows[1] - rows[0])


def kernel(doubles_hbm, singles_hbm, b_ref, out_ref, a, own, other, c, outer, doubles_ref, singles_ref, send_sem, recv_sem, local_sem):
    row, col = lax.axis_index("row"), lax.axis_index("col")
    zh, x, core = row // 8, lax.rem(row // 2, 4), lax.rem(row, 2)
    zl, y = col // 4, lax.rem(col, 4)
    zo = 1 - zl

    def at(dx=0, dy=0, dh=0, dl=0, dc=0):
        return (
            lax.rem(zh + dh, 2) * 8 + lax.rem(x + dx, 4) * 2 + lax.rem(core + dc, 2),
            lax.rem(zl + dl, 2) * 4 + lax.rem(y + dy, 4),
        )

    xs = [lax.rem(x + d, 4) for d in range(4)]
    ys = [lax.rem(y + d, 4) for d in range(4)]
    peers = [at(dx=1), at(dx=2), at(dx=3), at(dy=1), at(dy=3), at(dl=1), at(dh=1), at(dc=1)]

    bring = [
        pltpu.make_async_copy(doubles_hbm, doubles_ref, local_sem.at[14]),
        pltpu.make_async_copy(singles_hbm, singles_ref, local_sem.at[15]),
    ]
    for copy in bring[::-1]:
        copy.start()
    barrier = pltpu.get_barrier_semaphore()
    for peer in peers:
        pl.semaphore_signal(barrier, inc=1, device_id=peer, device_id_type=MESH)

    mine = pltpu.make_async_copy(b_ref, own.at[core], local_sem.at[0])
    mine.start()

    pairs, depth = doubles_ref.shape
    occupied = singles_ref.shape[0]
    first = (row * pairs) // occupied
    skip = lax.rem(row * pairs, occupied)
    lanes = lax.broadcasted_iota(jnp.int32, (1, depth), 1)
    bring[1].wait()
    for g in range(outer.shape[0] // occupied):
        line = singles_ref[pl.ds(jnp.minimum(first + g, occupied - 1), 1), :]
        factor = jnp.sum(jnp.where(lanes == col, line, 0.0), axis=1, keepdims=True)
        outer[pl.ds(g * occupied, occupied), :] = singles_ref[...] * factor
    bring[0].wait()
    a[x, y, zl, pl.ds(ROWS - 16, 16), :] = jnp.zeros((16, depth), jnp.bfloat16)
    for offset in range(0, occupied, math.gcd(pairs, occupied)):

        @pl.when(skip == offset)
        def _(offset=offset):
            tau = doubles_ref[...].astype(jnp.float32) + outer[pl.ds(offset, pairs), :]
            a[x, y, zl, pl.ds(0, pairs), :] = tau.astype(jnp.bfloat16)


    pl.semaphore_wait(barrier, len(peers))

    copies = []

    def send(src, dst, device):
        number = len(copies)
        copy = pltpu.make_async_remote_copy(
            src_ref=src,
            dst_ref=dst,
            send_sem=send_sem.at[number],
            recv_sem=recv_sem.at[number],
            device_id=device,
            device_id_type=MESH,
        )
        copy.start()
        copies.append(copy)
        return copy

    def send_a(index, rows, device):
        ref = a.at[index + (span(rows),)]
        return send(ref, ref, device)

    def arrive(started):
        for copy in started:
            copy.wait_recv()

    def y_start(dx, lo, rows):
        index = (xs[dx], ys[0], lo)
        return [send_a(index, rows, at(dy=1)), send_a(index, rows, at(dy=3))]

    def y_pass(started, dx, lo, rows, flip):
        up, down = HALVES[rows][::-1] if flip else HALVES[rows]
        arrive(started)
        return [
            send_a((xs[dx], ys[3], lo), up, at(dy=1)),
            send_a((xs[dx], ys[1], lo), down, at(dy=3)),
        ]

    def x_start(dy, lo, rows):
        index = (xs[0], ys[dy], lo)
        return [send_a(index, rows, at(dx=1)), send_a(index, rows, at(dx=3))]

    def x_pass(started, dy, lo, rows, flip):
        up, down = HALVES[rows][::-1] if flip else HALVES[rows]
        arrive(started)
        return [
            send_a((xs[3], ys[dy], lo), up, at(dx=1)),
            send_a((xs[1], ys[dy], lo), down, at(dx=3)),
        ]

    def product(left, right, where, cols):
        total = None
        for lo in range(2):
            for yy in range(4):
                term = jnp.dot(
                    left(yy, lo),
                    right[pl.ds((lo * 4 + yy) * DEPTH, DEPTH), :],
                    preferred_element_type=jnp.float32,
                )
                total = term if total is None else total + term
        total = total.astype(jnp.bfloat16)
        at_row = 0
        for dx, rows in where:
            count = rows[1] - rows[0]
            c[dx, span(rows), cols] = total[at_row : at_row + count]
            at_row += count

    def block(which, q, j=None):
        ref = which.at[q]
        return ref if j is None else ref.at[:, pl.ds(j * 128, 128)]

    def first_rows(dx, right, cols):
        product(lambda yy, lo: a[xs[dx], yy, lo, span(FIRST)], right, [(dx, FIRST)], cols)

    def second_rows(right, cols):
        product(
            lambda yy, lo: jnp.concatenate([a[xs[d], yy, lo, span(SECOND)] for d in range(4)], axis=0),
            right,
            [(d, SECOND) for d in range(4)],
            cols,
        )

    results = []
    kept = []

    def send_c(dx, rows, half, start, count):
        base = (lax.rem(zh + half, 2) * 8 + x * 2) * WIDTH + start
        dst = out_ref.at[span(rows), pl.ds(pl.multiple_of(base, 128), count)]
        src = c.at[dx, span(rows), pl.ds(half * 512 + start, count)]
        if dx:
            results.append(send(src, dst, at(dx=dx)))
        else:
            copy = pltpu.make_async_copy(src, dst, local_sem.at[1 + len(kept)])
            copy.start()
            kept.append(copy)

    def own_first(dx):
        @pl.loop(0, 2)
        def _(q):
            first_rows(dx, own.at[q], pl.ds(pl.multiple_of(q * WIDTH, WIDTH), WIDTH))

        send_c(dx, FIRST, 0, 0, 512)

    def other_first(dx, q, j=None):
        start, count = (q * 256, 256) if j is None else (q * 256 + j * 128, 128)
        first_rows(dx, block(other, q, j), pl.ds(512 + start, count))
        send_c(dx, FIRST, 1, start, count)

    def own_second():
        @pl.loop(0, 2)
        def _(q):
            second_rows(own.at[q], pl.ds(pl.multiple_of(q * WIDTH, WIDTH), WIDTH))

        for dx in (2, 1, 3, 0):
            send_c(dx, SECOND, 0, 0, 512)

    def other_second(q, j=None):
        start, count = (q * 256, 256) if j is None else (q * 256 + j * 128, 128)
        second_rows(block(other, q, j), pl.ds(512 + start, count))
        for dx in (2, 1, 3, 0):
            send_c(dx, SECOND, 1, start, count)

    half = own.shape[1] // 2
    part = pl.ds(pl.multiple_of(core * half, half), half)
    lane_block = {None: pl.ds(0, WIDTH), 0: pl.ds(0, 128), 1: pl.ds(128, 128)}

    def across(q, j):
        return send(own.at[q, part, lane_block[j]], other.at[q, part, lane_block[j]], at(dh=1))

    def share(started, q, j):
        started.wait_recv()
        ref = other.at[q, part, lane_block[j]]
        return send(ref, ref, at(dc=1))

    o, p = zl, zo
    pair = [send_a((xs[0], ys[0], zl), FIRST, at(dl=1)), send_a((xs[0], ys[0], zl), SECOND, at(dl=1))]
    sibling = send(b_ref, own.at[core], at(dc=1))
    xf = {}
    yf = {}
    x_o = x_start(0, o, FIRST)
    y_so = y_start(0, o, SECOND)
    y_0o = y_start(0, o, FIRST)
    xs_ = {}
    xt = {}
    xs_[0, 0] = x_start(0, o, SECOND)
    y_so2 = y_pass(y_so, 0, o, SECOND, False)
    mine.wait()
    sibling.wait_recv()
    za = across(0, None)
    x_o2 = x_pass(x_o, 0, o, FIRST, False)
    y_1o = y_start(1, o, FIRST)
    arrive(pair)
    x_p = x_start(0, p, FIRST)
    y_sp = y_start(0, p, SECOND)
    zb = across(1, 0)
    zc = across(1, 1)
    y_0o2 = y_pass(y_0o, 0, o, FIRST, False)
    xt[0, 0] = x_pass(xs_[0, 0], 0, o, SECOND, False)
    xs_[0, 1] = x_start(0, p, SECOND)
    arrive(x_o2)
    y_2o = y_start(2, o, FIRST)
    xs_[1, 0] = x_start(1, o, SECOND)
    xs_[3, 0] = x_start(3, o, SECOND)
    y_1o2 = y_pass(y_1o, 1, o, FIRST, False)
    x_p2 = x_pass(x_p, 0, p, FIRST, True)
    y_sp2 = y_pass(y_sp, 0, p, SECOND, True)
    xt[0, 1] = x_pass(xs_[0, 1], 0, p, SECOND, True)
    xs_[1, 1] = x_start(1, p, SECOND)
    xs_[3, 1] = x_start(3, p, SECOND)
    xt[1, 0] = x_pass(xs_[1, 0], 1, o, SECOND, False)
    xt[3, 0] = x_pass(xs_[3, 0], 3, o, SECOND, False)
    arrive(x_p2)
    y_2p = y_start(2, p, FIRST)
    y_2o2 = y_pass(y_2o, 2, o, FIRST, False)
    arrive(y_so2)
    xs_[2, 0] = x_start(2, o, SECOND)
    y_1p = y_start(1, p, FIRST)
    xt[1, 1] = x_pass(xs_[1, 1], 1, p, SECOND, True)
    xt[3, 1] = x_pass(xs_[3, 1], 3, p, SECOND, True)
    arrive(y_sp2)
    xs_[2, 1] = x_start(2, p, SECOND)
    y_2p2 = y_pass(y_2p, 2, p, FIRST, True)
    y_3o = y_start(3, o, FIRST)
    xt[2, 0] = x_pass(xs_[2, 0], 2, o, SECOND, False)
    xt[2, 1] = x_pass(xs_[2, 1], 2, p, SECOND, True)
    sa = share(za, 0, None)
    y_1p2 = y_pass(y_1p, 1, p, FIRST, True)
    y_3p = y_start(3, p, FIRST)
    for key in xt:
        arrive(xt[key])
    own_second()
    arrive(y_2o2 + y_2p2)
    own_first(2)
    sa.wait_recv()
    other_second(0)
    other_first(2, 0)
    y_3o2 = y_pass(y_3o, 3, o, FIRST, False)
    arrive(y_1o2 + y_1p2)
    own_first(1)
    other_first(1, 0)
    sb = share(zb, 1, 0)
    y_3p2 = y_pass(y_3p, 3, p, FIRST, True)
    y_0p = y_start(0, p, FIRST)
    sb.wait_recv()
    other_second(1, 0)
    other_first(2, 1, 0)
    other_first(1, 1, 0)
    arrive(y_3o2 + y_3p2)
    own_first(3)
    other_first(3, 0)
    other_first(3, 1, 0)
    y_0p2 = y_pass(y_0p, 0, p, FIRST, True)
    sc = share(zc, 1, 1)
    sc.wait_recv()
    other_first(3, 1, 1)
    other_second(1, 1)
    other_first(2, 1, 1)
    other_first(1, 1, 1)
    arrive(y_0o2 + y_0p2)
    own_first(0)
    other_first(0, 0)
    other_first(0, 1, 0)
    other_first(0, 1, 1)
    for copy in kept:
        copy.wait()
    arrive(results)
    for copy in copies:
        copy.wait_send()


def on_device(doubles, singles, integrals):
    rows = doubles.shape[0]
    depth, width = integrals.shape
    padded = pl.pallas_call(
        kernel,
        out_shape=jax.ShapeDtypeStruct((ROWS, 16 * width), jnp.bfloat16),
        in_specs=[
            pl.BlockSpec(memory_space=pltpu.HBM),
            pl.BlockSpec(memory_space=pltpu.HBM),
            pl.BlockSpec(memory_space=pltpu.HBM),
        ],
        out_specs=pl.BlockSpec(memory_space=pl.ANY),
        scratch_shapes=[
            pltpu.VMEM((4, 4, 2, ROWS, DEPTH), jnp.bfloat16),
            pltpu.VMEM((2, depth, width), jnp.bfloat16),
            pltpu.VMEM((2, depth, width), jnp.bfloat16),
            pltpu.VMEM((4, ROWS, 4 * width), jnp.bfloat16),
            pltpu.VMEM((300, DEPTH), jnp.float32),
            pltpu.VMEM(doubles.shape, doubles.dtype),
            pltpu.VMEM(singles.shape, singles.dtype),
            pltpu.SemaphoreType.DMA((128,)),
            pltpu.SemaphoreType.DMA((128,)),
            pltpu.SemaphoreType.DMA((16,)),
        ],
        compiler_params=pltpu.CompilerParams(
            collective_id=0, has_side_effects=True, vmem_limit_bytes=60 << 20
        ),
        cost_estimate=pl.CostEstimate(
            flops=2 * rows * depth * 16 * width, bytes_accessed=32 << 20, transcendentals=0
        ),
        name="ladder",
    )(doubles, singles, integrals)
    return padded[:rows]


def solution(mesh):
    return jax.shard_map(
        on_device,
        mesh=mesh,
        in_specs=(P("row", "col"), P(), P(None, ("col", "row"))),
        out_specs=P("row", "col"),
        check_vma=False,
    )
```

time: 81.5 us -> 73.5 us (0.902); the launches traced: 81.4 us -> 72.4 us
  Pallas kernels: 76.1 us -> 69.4 us
  local copies, waits for them, and re-layouts: 5.11 us -> 2.97 us
    pallas_call x1, Pallas kernels: 76.1 us -> 69.4 us  [on_device(): pl.pallas_call(kernel, out_shape=jax.ShapeDtypeStruct((ROWS, 16 * width),...]
    slice x0 -> x1, local copies, waits for them, and re-layouts: none -> 2.97 us  [on_device(): return padded[:rows]]
    unnamed x6 -> x0, local copies, waits for them, and re-layouts: 2.21 us -> none
    dynamic_slice x2 -> x0, local copies, waits for them, and re-layouts: 1.16 us -> none  [the longest x1 1.08 us: build_tau(): column = lax.dynamic_slice(singles, (0, col), (occupied, 1))]
    another operation x2 -> x0, local copies, waits for them, and re-layouts: 1.03 us -> none  [build_tau(): tiled = jnp.tile(singles, (pair_rows // occupied + 2, 1))]
where the time goes in v2:
time: 73.5 us; the launch traced here: 72.4 us
  Pallas kernels  69.4 us (94%)
  local copies, waits for them, and re-layouts  2.97 us (4%)
    pallas_call x1, Pallas kernels, on_device(): pl.pallas_call(kernel, out_shape=jax.ShapeDtypeStruct((ROWS, 16 * width),...  69.4 us
    slice x1, local copies, waits for them, and re-layouts, on_device(): return padded[:rows]  2.97 us

profile of v2, /device:TPU:0, one launch (start us, length us, event | category | flops | bytes accessed | tf_op | source)
XLA Modules:
  0.0 72.4 jit_solution(1795395833923221918)
XLA Ops:
  0.0 69.4 %ladder.1 = bf16[240,4096]{1,0:T(8,128)(2,1)} custom-call(bf16[225,480]{1,0:T(8,128)(2,1)} %doubles_hbm.1, f32[60,480]{1,0:T(8,128)} %singles_hbm.1, bf16[3840,256]{1,0:T(8,128)(2,1)} %b_ref.1), custom_call_target="tpu_custom_call" | custom-call | flops 7077888000 | bytes 33554432 | tf_op jit(solution)/shard_map/ladder/pallas_call | solution.py:307
  69.4 3.0 %slice.3 = bf16[225,4096]{1,0:T(8,128)(2,1)} slice(bf16[240,4096]{1,0:T(8,128)(2,1)} %ladder.1), slice={[0:225], [0:4096]} | slice | bytes 3686400 | tf_op jit(solution)/shard_map/slice | solution.py:336

commit v3 on v2

--- a/solution.py
+++ b/solution.py
@@ -15,14 +15,32 @@
 ALL = (0, ROWS)
 FIRST = (0, CUT)
 SECOND = (CUT, ROWS)
-HALVES = {FIRST: ((0, 96), (96, CUT)), SECOND: ((CUT, 208), (208, ROWS))}
+EARLY = (0, 96)
+LATE = (96, CUT)
+HALVES = {
+    FIRST: ((0, 96), (96, CUT)),
+    SECOND: ((CUT, 208), (208, ROWS)),
+    EARLY: ((0, 48), (48, 96)),
+    LATE: ((96, 144), (144, CUT)),
+}
+
+
+PIECES = ((0, None), (1, 0), (1, 1))
+ORDER = (
+    "pS", "ySo", "xFo", "pF", "sib", "ySp", "z0", "xS1o", "yS2o", "xS3o", "yF1o", "xF2o", "xFp", "z1", "yS2p",
+    "yF3o", "yF2o", "xS0o", "z2", "xS2o", "xF2p", "xS23o", "xS2p", "xS1p", "yF1p", "xS0p", "xS3p", "yF2p",
+    "xS20o", "xS22p", "yF22o", "xS21p", "yF21p", "xS22o", "xS20p", "xS21o", "xS23p", "yF22p", "s0", "yF3p",
+    "yF23o", "JSo", "yF21o", "JF2o", "yF23p", "yL", "yE", "s1", "JS0", "JF20", "JS1", "yF0p", "JF1o", "JF21",
+    "JF3o", "yL2", "JF10", "JF31", "yE2", "JF30", "s2", "JF11", "yF20p", "JF22", "JS2", "JF12", "JF32",
+    "JT10", "JT00", "JTo0", "JT22", "JTo1", "JT11", "JT01",
+)
 
 
 def span(rows):
     return pl.ds(rows[0], rows[1] - rows[0])
 
 
-def kernel(doubles_hbm, singles_hbm, b_ref, out_ref, a, own, other, c, outer, doubles_ref, singles_ref, send_sem, recv_sem, local_sem):
+def kernel(doubles_hbm, singles_hbm, b_ref, out_ref, a, own, other, c, acc, outer, doubles_ref, singles_ref, send_sem, recv_sem, local_sem):
     row, col = lax.axis_index("row"), lax.axis_index("col")
     zh, x, core = row // 8, lax.rem(row // 2, 4), lax.rem(row, 2)
     zl, y = col // 4, lax.rem(col, 4)
@@ -93,9 +111,13 @@
         ref = a.at[index + (span(rows),)]
         return send(ref, ref, device)
 
+    arrived = set()
+
     def arrive(started):
         for copy in started:
-            copy.wait_recv()
+            if id(copy) not in arrived:
+                arrived.add(id(copy))
+                copy.wait_recv()
 
     def y_start(dx, lo, rows):
         index = (xs[dx], ys[0], lo)
@@ -138,6 +160,37 @@
             c[dx, span(rows), cols] = total[at_row : at_row + count]
             at_row += count
 
+    def own_terms(piece, chunks, stage):
+        half, start, count = (0, 0, 512) if piece is None else (1, *columns_of(*piece))
+        which = other if half else own
+        width = min(count, WIDTH)
+
+        def part_of(q, first):
+            cols = pl.ds(half * 512 + start + first, width)
+            total = acc[:, cols] if stage == 1 else None
+            for yy, lo in chunks:
+                term = jnp.dot(
+                    a[x, yy, lo, span(FIRST)],
+                    which[q, pl.ds(pl.multiple_of((lo * 4 + yy) * DEPTH, 16), DEPTH), pl.ds(start % WIDTH, width)],
+                    preferred_element_type=jnp.float32,
+                )
+                total = term if total is None else total + term
+            if stage:
+                c[0, span(FIRST), cols] = total.astype(jnp.bfloat16)
+            else:
+                acc[:, cols] = total
+
+        if piece is None:
+            part_of(0, 0)
+            part_of(1, WIDTH)
+        else:
+            part_of(piece[0], 0)
+        if stage:
+            send_c(0, FIRST, half, start, count)
+
+    def columns_of(q, j):
+        return (q * 256, 256) if j is None else (q * 256 + j * 128, 128)
+
     def block(which, q, j=None):
         ref = which.at[q]
         return ref if j is None else ref.at[:, pl.ds(j * 128, 128)]
@@ -201,99 +254,129 @@
         return send(own.at[q, part, lane_block[j]], other.at[q, part, lane_block[j]], at(dh=1))
 
     def share(started, q, j):
-        started.wait_recv()
+        arrive([started])
         ref = other.at[q, part, lane_block[j]]
         return send(ref, ref, at(dc=1))
 
-    o, p = zl, zo
-    pair = [send_a((xs[0], ys[0], zl), FIRST, at(dl=1)), send_a((xs[0], ys[0], zl), SECOND, at(dl=1))]
+    done = {}
+    los = {"o": zl, "p": zo}
+
+    def need(*names):
+        for name in names:
+            arrive(done[name])
+
+    def first_ready(dx, lo):
+        if dx == 2:
+            need("xF2" + lo)
+        elif dx:
+            need("xF" + lo)
+        elif lo == "p":
+            need("pF")
+
+    def second_ready(dy, lo):
+        if dy == 2:
+            need("yS2" + lo)
+        elif dy:
+            need("yS" + lo)
+        elif lo == "p":
+            need("pS")
+
+    def all_second():
+        need("pS", "ySo", "ySp", "yS2o", "yS2p")
+        for lo in "op":
+            for dy in "0123":
+                need("xS" + dy + lo, "xS2" + dy + lo)
+
+    def all_first(dx):
+        for lo in "op":
+            if dx == 2:
+                need("xF2" + lo)
+            elif dx:
+                need("xF" + lo)
+            need("yF" + str(dx) + lo, "yF2" + str(dx) + lo)
+
+    def columns_ready(which):
+        if which == "o":
+            need("sib")
+        elif which == "0":
+            need("z0", "s0")
+        else:
+            need("z1", "s1") if which == "1" else need("z2", "s2")
+
+    def run(name):
+        kind, rest = name[:2], name[2:]
+        out = []
+        if name == "sib":
+            mine.wait()
+            out = [sibling]
+        elif kind == "pF":
+            out = [send_a((xs[0], ys[0], zl), FIRST, at(dl=1))]
+        elif kind == "pS":
+            out = [send_a((xs[0], ys[0], zl), SECOND, at(dl=1))]
+        elif name[0] == "z":
+            need("sib")
+            out = [across(*PIECES[int(name[1])])]
+        elif name[0] == "s":
+            out = [share(done["z" + name[1]][0], *PIECES[int(name[1])])]
+        elif name in ("yE", "yL"):
+            out = y_start(0, zl, EARLY if name == "yE" else LATE)
+        elif name in ("yE2", "yL2"):
+            need(name[:2])
+            out = y_pass(done[name[:2]], 0, zl, EARLY if name == "yE2" else LATE, False)
+        elif kind == "xF":
+            lo = name[-1]
+            if rest[0] == "2":
+                out = x_pass(done["xF" + lo], 0, los[lo], FIRST, lo == "p")
+            else:
+                first_ready(0, lo)
+                out = x_start(0, los[lo], FIRST)
+        elif kind == "yF":
+            lo, dx = name[-1], int(name[-2])
+            if len(rest) == 3:
+                out = y_pass(done["yF" + rest[1:]], dx, los[lo], FIRST, lo == "p")
+            else:
+                first_ready(dx, lo)
+                out = y_start(dx, los[lo], FIRST)
+        elif kind == "yS":
+            lo = name[-1]
+            if rest[0] == "2":
+                out = y_pass(done["yS" + lo], 0, los[lo], SECOND, lo == "p")
+            else:
+                second_ready(0, lo)
+                out = y_start(0, los[lo], SECOND)
+        elif kind == "xS":
+            lo, dy = name[-1], int(name[-2])
+            if len(rest) == 3:
+                out = x_pass(done["xS" + rest[1:]], dy, los[lo], SECOND, lo == "p")
+            else:
+                second_ready(dy, lo)
+                out = x_start(dy, los[lo], SECOND)
+        elif kind == "JS":
+            all_second()
+            columns_ready(rest)
+            own_second() if rest == "o" else other_second(*PIECES["012".index(rest)])
+        elif kind == "JF":
+            dx = int(rest[0])
+            all_first(dx)
+            columns_ready(rest[1])
+            own_first(dx) if rest[1] == "o" else other_first(dx, *PIECES["012".index(rest[1])])
+        elif kind == "JT":
+            stage = int(rest[1])
+            piece = None if rest[0] == "o" else PIECES["012".index(rest[0])]
+            need("pF", "yE", "yE2", "yL", "yL2", "yF0p")
+            columns_ready(rest[0])
+            early = [(ys[d], zl) for d in (0, 1, 3, 2)] + [(ys[d], zo) for d in (0, 1, 3)]
+            final = [(ys[2], zo)]
+            if stage:
+                need("yF20p")
+            if stage == 1:
+                need("JT" + rest[0] + "0")
+            own_terms(piece, (early, final, early + final)[stage], stage)
+        done[name] = out
+
     sibling = send(b_ref, own.at[core], at(dc=1))
-    xf = {}
-    yf = {}
-    x_o = x_start(0, o, FIRST)
-    y_so = y_start(0, o, SECOND)
-    y_0o = y_start(0, o, FIRST)
-    xs_ = {}
-    xt = {}
-    xs_[0, 0] = x_start(0, o, SECOND)
-    y_so2 = y_pass(y_so, 0, o, SECOND, False)
-    mine.wait()
-    sibling.wait_recv()
-    za = across(0, None)
-    x_o2 = x_pass(x_o, 0, o, FIRST, False)
-    y_1o = y_start(1, o, FIRST)
-    arrive(pair)
-    x_p = x_start(0, p, FIRST)
-    y_sp = y_start(0, p, SECOND)
-    zb = across(1, 0)
-    zc = across(1, 1)
-    y_0o2 = y_pass(y_0o, 0, o, FIRST, False)
-    xt[0, 0] = x_pass(xs_[0, 0], 0, o, SECOND, False)
-    xs_[0, 1] = x_start(0, p, SECOND)
-    arrive(x_o2)
-    y_2o = y_start(2, o, FIRST)
-    xs_[1, 0] = x_start(1, o, SECOND)
-    xs_[3, 0] = x_start(3, o, SECOND)
-    y_1o2 = y_pass(y_1o, 1, o, FIRST, False)
-    x_p2 = x_pass(x_p, 0, p, FIRST, True)
-    y_sp2 = y_pass(y_sp, 0, p, SECOND, True)
-    xt[0, 1] = x_pass(xs_[0, 1], 0, p, SECOND, True)
-    xs_[1, 1] = x_start(1, p, SECOND)
-    xs_[3, 1] = x_start(3, p, SECOND)
-    xt[1, 0] = x_pass(xs_[1, 0], 1, o, SECOND, False)
-    xt[3, 0] = x_pass(xs_[3, 0], 3, o, SECOND, False)
-    arrive(x_p2)
-    y_2p = y_start(2, p, FIRST)
-    y_2o2 = y_pass(y_2o, 2, o, FIRST, False)
-    arrive(y_so2)
-    xs_[2, 0] = x_start(2, o, SECOND)
-    y_1p = y_start(1, p, FIRST)
-    xt[1, 1] = x_pass(xs_[1, 1], 1, p, SECOND, True)
-    xt[3, 1] = x_pass(xs_[3, 1], 3, p, SECOND, True)
-    arrive(y_sp2)
-    xs_[2, 1] = x_start(2, p, SECOND)
-    y_2p2 = y_pass(y_2p, 2, p, FIRST, True)
-    y_3o = y_start(3, o, FIRST)
-    xt[2, 0] = x_pass(xs_[2, 0], 2, o, SECOND, False)
-    xt[2, 1] = x_pass(xs_[2, 1], 2, p, SECOND, True)
-    sa = share(za, 0, None)
-    y_1p2 = y_pass(y_1p, 1, p, FIRST, True)
-    y_3p = y_start(3, p, FIRST)
-    for key in xt:
-        arrive(xt[key])
-    own_second()
-    arrive(y_2o2 + y_2p2)
-    own_first(2)
-    sa.wait_recv()
-    other_second(0)
-    other_first(2, 0)
-    y_3o2 = y_pass(y_3o, 3, o, FIRST, False)
-    arrive(y_1o2 + y_1p2)
-    own_first(1)
-    other_first(1, 0)
-    sb = share(zb, 1, 0)
-    y_3p2 = y_pass(y_3p, 3, p, FIRST, True)
-    y_0p = y_start(0, p, FIRST)
-    sb.wait_recv()
-    other_second(1, 0)
-    other_first(2, 1, 0)
-    other_first(1, 1, 0)
-    arrive(y_3o2 + y_3p2)
-    own_first(3)
-    other_first(3, 0)
-    other_first(3, 1, 0)
-    y_0p2 = y_pass(y_0p, 0, p, FIRST, True)
-    sc = share(zc, 1, 1)
-    sc.wait_recv()
-    other_first(3, 1, 1)
-    other_second(1, 1)
-    other_first(2, 1, 1)
-    other_first(1, 1, 1)
-    arrive(y_0o2 + y_0p2)
-    own_first(0)
-    other_first(0, 0)
-    other_first(0, 1, 0)
-    other_first(0, 1, 1)
+    for name in ORDER:
+        run(name)
     for copy in kept:
         copy.wait()
     arrive(results)
@@ -318,6 +401,7 @@
             pltpu.VMEM((2, depth, width), jnp.bfloat16),
             pltpu.VMEM((2, depth, width), jnp.bfloat16),
             pltpu.VMEM((4, ROWS, 4 * width), jnp.bfloat16),
+            pltpu.VMEM((CUT, 4 * width), jnp.float32),
             pltpu.VMEM((300, DEPTH), jnp.float32),
             pltpu.VMEM(doubles.shape, doubles.dtype),
             pltpu.VMEM(singles.shape, singles.dtype),

time: 73.5 us -> 70.1 us (0.954); the launches traced: 72.4 us -> 70 us
  Pallas kernels: 69.4 us -> 67 us
    pallas_call x1, Pallas kernels: 69.4 us -> 67 us  [on_device(): pl.pallas_call(kernel, out_shape=jax.ShapeDtypeStruct((ROWS, 16 * width),...]
where the time goes in v3:
time: 70.1 us; the launch traced here: 70 us
  Pallas kernels  67 us (96%)
  local copies, waits for them, and re-layouts  2.97 us (4%)
    pallas_call x1, Pallas kernels, on_device(): pl.pallas_call(kernel, out_shape=jax.ShapeDtypeStruct((ROWS, 16 * width),...  67 us
    slice x1, local copies, waits for them, and re-layouts, on_device(): return padded[:rows]  2.97 us

profile of v3, /device:TPU:0, one launch (start us, length us, event | category | flops | bytes accessed | tf_op | source)
XLA Modules:
  0.0 70.0 jit_solution(18134502321666129484)
XLA Ops:
  0.0 67.0 %ladder.1 = bf16[240,4096]{1,0:T(8,128)(2,1)} custom-call(bf16[225,480]{1,0:T(8,128)(2,1)} %doubles_hbm.1, f32[60,480]{1,0:T(8,128)} %singles_hbm.1, bf16[3840,256]{1,0:T(8,128)(2,1)} %b_ref.1), custom_call_target="tpu_custom_call" | custom-call | flops 7077888000 | bytes 33554432 | tf_op jit(solution)/shard_map/ladder/pallas_call | solution.py:390
  67.0 3.0 %slice.3 = bf16[225,4096]{1,0:T(8,128)(2,1)} slice(bf16[240,4096]{1,0:T(8,128)(2,1)} %ladder.1), slice={[0:225], [0:4096]} | slice | bytes 3686400 | tf_op jit(solution)/shard_map/slice | solution.py:420

commit v4 on v3

--- a/solution.py
+++ b/solution.py
@@ -247,16 +247,24 @@
             send_c(dx, SECOND, 1, start, count)
 
     half = own.shape[1] // 2
-    part = pl.ds(pl.multiple_of(core * half, half), half)
     lane_block = {None: pl.ds(0, WIDTH), 0: pl.ds(0, 128), 1: pl.ds(128, 128)}
 
+    def parts_of(q, j):
+        count = 2 if (q, j) == PIECES[-1] else 1
+        rows = half // count
+        return [pl.ds(pl.multiple_of(core * half + k * rows, rows), rows) for k in range(count)]
+
     def across(q, j):
-        return send(own.at[q, part, lane_block[j]], other.at[q, part, lane_block[j]], at(dh=1))
+        lanes = lane_block[j]
+        return [send(own.at[q, rows, lanes], other.at[q, rows, lanes], at(dh=1)) for rows in parts_of(q, j)]
 
     def share(started, q, j):
-        arrive([started])
-        ref = other.at[q, part, lane_block[j]]
-        return send(ref, ref, at(dc=1))
+        out = []
+        for copy, rows in zip(started, parts_of(q, j)):
+            arrive([copy])
+            ref = other.at[q, rows, lane_block[j]]
+            out.append(send(ref, ref, at(dc=1)))
+        return out
 
     done = {}
     los = {"o": zl, "p": zo}
@@ -315,9 +323,9 @@
             out = [send_a((xs[0], ys[0], zl), SECOND, at(dl=1))]
         elif name[0] == "z":
             need("sib")
-            out = [across(*PIECES[int(name[1])])]
+            out = across(*PIECES[int(name[1])])
         elif name[0] == "s":
-            out = [share(done["z" + name[1]][0], *PIECES[int(name[1])])]
+            out = share(done["z" + name[1]], *PIECES[int(name[1])])
         elif name in ("yE", "yL"):
             out = y_start(0, zl, EARLY if name == "yE" else LATE)
         elif name in ("yE2", "yL2"):

time: 70.1 us -> 70.1 us (level)
  no operation moved by 1% of the time
where the time goes in v4:
time: 70.1 us; the launch traced here: 70 us
  Pallas kernels  67 us (96%)
  local copies, waits for them, and re-layouts  2.97 us (4%)
    pallas_call x1, Pallas kernels, on_device(): pl.pallas_call(kernel, out_shape=jax.ShapeDtypeStruct((ROWS, 16 * width),...  67 us
    slice x1, local copies, waits for them, and re-layouts, on_device(): return padded[:rows]  2.97 us

profile of v4, /device:TPU:0, one launch (start us, length us, event | category | flops | bytes accessed | tf_op | source)
XLA Modules:
  0.0 70.0 jit_solution(4646293403459496915)
XLA Ops:
  0.0 67.0 %ladder.1 = bf16[240,4096]{1,0:T(8,128)(2,1)} custom-call(bf16[225,480]{1,0:T(8,128)(2,1)} %doubles_hbm.1, f32[60,480]{1,0:T(8,128)} %singles_hbm.1, bf16[3840,256]{1,0:T(8,128)(2,1)} %b_ref.1), custom_call_target="tpu_custom_call" | custom-call | flops 7077888000 | bytes 33554432 | tf_op jit(solution)/shard_map/ladder/pallas_call | solution.py:398
  67.0 3.0 %slice.3 = bf16[225,4096]{1,0:T(8,128)(2,1)} slice(bf16[240,4096]{1,0:T(8,128)(2,1)} %ladder.1), slice={[0:225], [0:4096]} | slice | bytes 3686400 | tf_op jit(solution)/shard_map/slice | solution.py:428
